TPU v7x, 32 devices: a whole 2x2x4 slice. The times are simulated.
32 devices in a mesh: groups: 2 (over y), seq: 4 (over z), head: 2 (over x), sub: 2 (over core).
Axes of the slice: x: 2, y: 2, z: 4, core: 2. Of those that a mesh axis runs over, the one named last changes fastest.
Arguments:
- queries: bfloat16 [8192, 2560], P(('groups', 'seq'), 'head'), parts along dimension 0, may hold values from -8 to 8
- cur_keys: bfloat16 [8192, 2560], P(('groups', 'seq', 'sub'), 'head'), parts along dimension 0, may hold values from -8 to 8
- cur_values: bfloat16 [8192, 2560], P(('groups', 'seq', 'sub'), 'head'), parts along dimension 0, may hold values from -6 to 6
- mem_keys: bfloat16 [256, 64, 2560], P(('groups', 'seq', 'sub'), None, 'head'), parts along dimension 0, may hold values from -6.5 to 6.5
- mem_values: bfloat16 [256, 64, 2560], P(('groups', 'seq', 'sub'), None, 'head'), parts along dimension 0, may hold values from -6 to 6
- frame_ids: int32 [8, 8], P('groups'), parts along dimension 0, may hold values from 0 to 127, as said below
- frame_counts: int32 [256], P('groups'), parts along dimension 0, may hold values from 1 to 64, as said below
- out_weight: bfloat16 [2560, 5120], P('head', 'sub'), may hold values from -0.125 to 0.125
Outputs:
- projected: bfloat16 [8192, 5120], P(('groups', 'seq', 'head'), 'sub'), parts along dimension 0
There are 2 independent parts, one for each index of `groups`. A program takes and returns all parts, laid end to end along the dimension named above; an argument that names none is the same for every part. Nothing has to cross between parts.
Inputs may be any that keep to these rules, and one draw needn't show every extreme that they name: `frame_ids`: row c lists the 8 memory frames retrieved for stretch c; frame f is held by owner f // 16, and the 8 frames of a row lie on 8 different owners, one on each. Frame f has its first frame_counts[f] token slots valid; the other slots are padding.
All inputs are finite; a program needn't handle non-finite values.
Results may differ from a plain program's by a relative error of at most 0.009.
Values may be sent and summed in bfloat16 or wider, within the bound.
No kernel may reach another device: no remote copies, remote signals or barrier semaphores. Data moves between devices by JAX's collectives and lax.ppermute only.
A program may use at most 192 MiB of HBM per device.

v0:
```python
import functools
import math

import jax
import jax.numpy as jnp
from jax import lax
from jax.experimental import pallas as pl
from jax.experimental.pallas import tpu as pltpu
from jax.sharding import PartitionSpec as P

HD = 128
FT = 64
FR_DEV = 16
F32 = jnp.float32
BF16 = jnp.bfloat16
EXP2_SCALE = math.log2(math.e) / math.sqrt(HD)
MASKED = -1e30
VMEM_LIMIT = 24 * 1024 * 1024
SWAP = [(0, 1), (1, 0)]
SHORT = pl.CostEstimate(flops=1024, bytes_accessed=1024, transcendentals=0)
ANY = pl.BlockSpec(memory_space=pl.ANY)
HBM = pl.BlockSpec(memory_space=pltpu.HBM)
VMEM = pl.BlockSpec(memory_space=pltpu.VMEM)


def params():
    return pltpu.CompilerParams(vmem_limit_bytes=VMEM_LIMIT)


def in_hbm(array):
    return pltpu.with_memory_space_constraint(array, pltpu.HBM)


def in_vmem(array):
    return pltpu.with_memory_space_constraint(array, pltpu.VMEM)


def quarter(other_seq, other_group):
    seq_part = lax.rem(lax.axis_index("seq"), 2)
    group = lax.axis_index("groups")
    return 2 * (1 - seq_part if other_seq else seq_part) + (1 - group if other_group else group)


def copy_all(pairs, sems):
    copies = [pltpu.make_async_copy(*pair, sems.at[index]) for index, pair in enumerate(pairs)]
    for copy in copies:
        copy.start()
    for copy in copies:
        copy.wait()


def held_by(ids, stretch, owner, count):
    found = jnp.int32(0)
    for entry in range(count):
        frame = ids[stretch, entry]
        slot = frame - owner * FR_DEV
        found = jnp.where((slot >= 0) & (slot < FR_DEV), frame, found)
    return found


def pack_kernel(seq_count, parts, ids, keys, values, cur_keys, cur_values, *rest):
    outs = rest[:seq_count]
    sibling, sems = rest[seq_count:]
    seq_index = lax.axis_index("seq")
    sub_index = lax.axis_index("sub")
    width = sibling.shape[1]
    count = cur_keys.shape[0]
    frame_count = 2 * seq_count

    def columns_of(half):
        return pl.ds(pl.multiple_of(half * width, 128), width)

    pairs = []
    for shift, out in enumerate(outs):
        owner = seq_index * 2 + sub_index
        wanted = held_by(ids, lax.rem(seq_index + shift, seq_count), owner, frame_count) - owner * FR_DEV
        for turn in range(2):
            half = sub_index if turn == 0 else 1 - sub_index
            for part, source in enumerate((keys, values)):
                if shift == 0 and turn == 1:
                    target = sibling.at[pl.ds(2 * count + part * FT, FT), :]
                else:
                    target = out.at[pl.ds((2 * turn + part) * FT, FT), :]
                pairs.append((source.at[wanted, :, columns_of(half)], target))
    rows = count // parts
    for part, source in enumerate((cur_keys, cur_values)):
        for low_row in range(0, count, rows):
            target = sibling.at[pl.ds(part * count + low_row, rows), :]
            pairs.append((source.at[pl.ds(low_row, rows), columns_of(1 - sub_index)], target))
    copy_all(pairs, sems)


def pack(frame_ids, mem_keys, mem_values, cur_keys, cur_values, seq_count):
    parts = 4
    width = mem_keys.shape[2] // 2
    rows = [2 * FT] + [4 * FT] * (seq_count - 1) + [2 * cur_keys.shape[0] + 2 * FT]
    shapes = [(count, width) for count in rows]
    return pl.pallas_call(
        functools.partial(pack_kernel, seq_count, parts),
        out_shape=[pltpu.VMEM(shape, BF16) for shape in shapes],
        in_specs=[pl.BlockSpec(memory_space=pltpu.SMEM)] + [HBM] * 4,
        out_specs=[VMEM] * len(shapes),
        scratch_shapes=[pltpu.SemaphoreType.DMA((4 * seq_count + 2 * parts,))],
        compiler_params=params(),
        name="pack",
        cost_estimate=pl.CostEstimate(flops=0, bytes_accessed=12 * 2**20, transcendentals=0),
    )(*map(in_hbm, (frame_ids, mem_keys, mem_values, cur_keys, cur_values)))


def pack_columns_kernel(low, parts, weight, after, out, sems):
    first = pl.multiple_of(low + quarter(False, False) * out.shape[1], 128)
    rows = weight.shape[0] // parts
    spans = [pl.ds(part * rows, rows) for part in range(parts)]
    copy_all([(weight.at[span, pl.ds(first, out.shape[1])], out.at[span, :]) for span in spans], sems)


def pack_columns(weight, low, share, after):
    parts = 8
    return pl.pallas_call(
        functools.partial(pack_columns_kernel, low, parts),
        out_shape=pltpu.VMEM((weight.shape[0], share), BF16),
        in_specs=[HBM, ANY],
        out_specs=VMEM,
        scratch_shapes=[pltpu.SemaphoreType.DMA((parts,))],
        compiler_params=params(),
        name="pack_columns",
        cost_estimate=SHORT,
    )(in_hbm(weight), in_vmem(after))


def pass_on_kernel(*refs):
    arrays, out = refs[:-2], refs[-1]
    rows = out.shape[0] // len(arrays)
    for index, array in enumerate(arrays):
        out[pl.ds(index * rows, rows), :] = array[pl.ds(rows, rows), :]


def pass_on(arrays, after):
    rows, width = arrays[0].shape
    return pl.pallas_call(
        pass_on_kernel,
        out_shape=pltpu.VMEM((len(arrays) * rows // 2, width), BF16),
        in_specs=[VMEM] * len(arrays) + [ANY],
        out_specs=VMEM,
        compiler_params=params(),
        name="pass_on",
        cost_estimate=SHORT,
    )(*map(in_vmem, arrays), in_vmem(after))


def load_kernel(parts, seq_count, ids, counts, weight, after, out, mask, sems):
    rows = weight.shape[0] // parts
    spans = [pl.ds(part * rows, rows) for part in range(parts)]
    copies = [pltpu.make_async_copy(weight.at[span, :], out.at[span, :], sems.at[index]) for index, span in enumerate(spans)]
    for copy in copies:
        copy.start()
    seq_index = lax.axis_index("seq")
    sub_index = lax.axis_index("sub")
    slot = lax.broadcasted_iota(jnp.int32, (1, FT), 1)
    for index in range(2 * seq_count):
        turn, shift = divmod(index, seq_count)
        source = lax.rem(seq_index + seq_count - shift, seq_count) * 2
        owner = source + (sub_index if turn == 0 else 1 - sub_index)
        live = slot < counts[held_by(ids, seq_index, owner, 2 * seq_count)]
        mask[pl.ds(index, 1), :] = jnp.where(live, 0.0, MASKED).astype(F32)
    for copy in copies:
        copy.wait()


def load(frame_ids, frame_counts, weight, seq_count, after):
    parts = 8
    return pl.pallas_call(
        functools.partial(load_kernel, parts, seq_count),
        out_shape=[pltpu.VMEM(weight.shape, BF16), pltpu.VMEM((2 * seq_count, FT), F32)],
        in_specs=[pl.BlockSpec(memory_space=pltpu.SMEM)] * 2 + [HBM, ANY],
        out_specs=[VMEM, VMEM],
        scratch_shapes=[pltpu.SemaphoreType.DMA((parts,))],
        compiler_params=params(),
        name="load",
        cost_estimate=pl.CostEstimate(flops=0, bytes_accessed=2 * weight.size, transcendentals=0),
    )(*map(in_hbm, (frame_ids, frame_counts, weight)), in_vmem(after))


def gate(array, after):
    return pl.pallas_call(
        lambda *refs: None,
        in_specs=[ANY, ANY],
        out_specs=ANY,
        out_shape=jax.ShapeDtypeStruct(array.shape, array.dtype),
        input_output_aliases={0: 0},
        compiler_params=params(),
        name="gate",
        cost_estimate=SHORT,
    )(in_vmem(array), in_vmem(after))


def copied_kernel(array, after, out):
    out[...] = array[...]


def copied(array, after):
    return pl.pallas_call(
        copied_kernel,
        in_specs=[VMEM, ANY],
        out_specs=VMEM,
        out_shape=pltpu.VMEM(array.shape, array.dtype),
        compiler_params=params(),
        name="copied",
        cost_estimate=SHORT,
    )(in_vmem(array), in_vmem(after))


def dot_t(left, right):
    return lax.dot_general(left, right, (((1,), (1,)), ((), ())), preferred_element_type=F32)


def wide(column, count):
    return jnp.concatenate([column] * count, axis=1)


def with_ones(values):
    return jnp.concatenate([values, jnp.ones_like(values)], axis=1)


def current_kernel(step, queries, own_keys, own_values, sibling, out, lse, q, own_k, own_v, sems):
    heads, rows, _ = out.shape
    count = own_k.shape[0]
    half = pl.ds(pl.multiple_of(lax.axis_index("sub") * q.shape[1], 128), q.shape[1])
    copy_all(
        [(queries.at[:, half], q), (own_keys.at[:, half], own_k), (own_values.at[:, half], own_v)],
        sems,
    )

    @pl.loop(0, heads)
    def _(head):
        columns = pl.ds(pl.multiple_of(head * HD, HD), HD)
        keys = jnp.concatenate([own_k[:, columns], sibling[pl.ds(0, count), columns]], axis=0)
        values = with_ones(jnp.concatenate([own_v[:, columns], sibling[pl.ds(count, count), columns]], axis=0))
        for low in range(0, rows, step):
            span = pl.ds(low, step)
            scores = dot_t(q[span, columns], keys)
            row_max = jnp.broadcast_to(jnp.max(scores, axis=1, keepdims=True), (step, HD))
            weights = jnp.exp2((scores - wide(row_max, 2 * count // HD)) * EXP2_SCALE).astype(BF16)
            product = jnp.dot(weights, values, preferred_element_type=F32)
            total = product[:, HD:]
            out[head, span, :] = product[:, :HD] / total
            lse[head, span, :] = row_max * EXP2_SCALE + jnp.log2(total)


def attend_current(queries, cur_keys, cur_values, sibling, heads):
    rows = queries.shape[0]
    keys = cur_keys.shape[0]
    return pl.pallas_call(
        functools.partial(current_kernel, 512),
        in_specs=[HBM] * 3 + [VMEM],
        out_specs=[VMEM] * 3,
        out_shape=[pltpu.VMEM((heads, rows, HD), F32)] * 2 + [pltpu.VMEM((rows, heads * HD), BF16)],
        scratch_shapes=[pltpu.VMEM((keys, heads * HD), BF16)] * 2 + [pltpu.SemaphoreType.DMA((3,))],
        compiler_params=params(),
        name="attend_current",
        cost_estimate=pl.CostEstimate(
            flops=60 * heads * rows * 2 * keys * HD, bytes_accessed=heads * rows * HD * 12, transcendentals=heads * rows * 2 * keys
        ),
    )(in_hbm(queries), in_hbm(cur_keys), in_hbm(cur_values), in_vmem(sibling))


def frames_kernel(heads, half_of, state_half_of, first, starts, final, bias, q, held, lse, *rest):
    frames = rest[: len(starts)]
    outs = rest[-1:] if final else rest[-2:]
    count, rows = len(starts), outs[0].shape[-2]

    def rows_of(half):
        return pl.ds(pl.multiple_of(half() * rows, rows), rows)

    span, state_span = rows_of(half_of), rows_of(state_half_of)
    mask = jnp.concatenate([bias[pl.ds(first + index, 1), :] for index in range(count)], axis=1)

    def gathered(head, part):
        columns = pl.ds(head * HD, HD)
        return jnp.concatenate(
            [frame[pl.ds(start + part * FT, FT), columns] for frame, start in zip(frames, starts)], axis=0
        )

    def scores_of(head):
        return dot_t(q[span, pl.ds(head * HD, HD)], gathered(head, 0))

    def finish(head, scores):
        scores = scores * EXP2_SCALE + mask
        old = lse[head, state_span, :]
        new_max = jnp.maximum(old, jnp.max(scores, axis=1, keepdims=True))
        weights = jnp.exp2(scores - wide(new_max, count * FT // HD)).astype(BF16)
        product = jnp.dot(weights, with_ones(gathered(head, 1)), preferred_element_type=F32)
        scale = jnp.exp2(old - new_max)
        total = scale + product[:, HD:]
        top = (held[head, state_span, :] * scale + product[:, :HD]) / total
        if final:
            outs[0][:, pl.ds(head * HD, HD)] = top.astype(BF16)
        else:
            outs[0][head] = top
            outs[1][head] = new_max + jnp.log2(total)

    scores = scores_of(0)
    for head in range(heads):
        following = scores_of(head + 1) if head + 1 < heads else None
        finish(head, scores)
        scores = following


def far_half():
    return 1 - lax.axis_index("head")


def near_half():
    return lax.axis_index("head")


def attend_frames(name, half, bias, first, q, held, lse, frames, starts, final, after=()):
    heads, state_rows, _ = held.shape
    rows = q.shape[0] // 2
    state_half = half if state_rows > rows else lambda: jnp.int32(0)
    operands = [bias, q, held, lse, *frames]
    if final:
        out_shape = [pltpu.VMEM((rows, heads * HD), BF16)]
    else:
        out_shape = [pltpu.VMEM((heads, rows, HD), F32)] * 2
    outs = pl.pallas_call(
        functools.partial(frames_kernel, heads, half, state_half, first, tuple(starts), final),
        in_specs=[VMEM] * len(operands) + [ANY] * len(after),
        out_specs=[VMEM] * len(out_shape),
        out_shape=out_shape,
        compiler_params=params(),
        name=name,
        cost_estimate=SHORT,
    )(*map(in_vmem, operands), *map(in_vmem, after))
    return outs[0] if final else outs


def both(mine, other):
    first, second = mine[...], other[...]
    return jnp.where(
        lax.axis_index("sub") == 0,
        jnp.concatenate([first, second], axis=1),
        jnp.concatenate([second, first], axis=1),
    )


def project_kernel(step, mine, other, weight, *rest):
    out = rest[-1]
    rows = both(mine, other)

    @pl.loop(0, out.shape[1] // step)
    def _(index):
        columns = pl.ds(pl.multiple_of(index * step, step), step)
        out[:, columns] = jnp.dot(rows, weight[:, columns], preferred_element_type=F32).astype(BF16)


def unshared_columns(low, share):
    return pl.ds(0, low), pl.ds(pl.multiple_of(low + quarter(True, True) * share, 128), share)


def unshared_kernel(low, mine, other, weight, *rest):
    out = rest[-1]
    rows = both(mine, other)
    start = 0
    for columns in unshared_columns(low, out.shape[1] - low):
        out[:, pl.ds(start, columns.size)] = jnp.dot(rows, weight[:, columns], preferred_element_type=F32).astype(BF16)
        start += columns.size


def project_call(kernel, name, mine, other, weight, width, after):
    return pl.pallas_call(
        kernel,
        in_specs=[VMEM] * 3 + [ANY] * len(after),
        out_specs=VMEM,
        out_shape=pltpu.VMEM((mine.shape[0], width), BF16),
        compiler_params=params(),
        name=name,
        cost_estimate=SHORT,
    )(*map(in_vmem, (mine, other, weight, *after)))


def project(mine, other, weight, after):
    return project_call(functools.partial(project_kernel, 512), "project", mine, other, weight, weight.shape[1], after)


def project_unshared(mine, other, weight, low, share, after):
    kernel = functools.partial(unshared_kernel, low)
    return project_call(kernel, "project_unshared", mine, other, weight, low + share, after)


def write_blocks(blocks, out, scratch, sems):
    copies, start = [], 0
    for index, (block, low) in enumerate(blocks):
        span = pl.ds(start, block.shape[1])
        scratch[:, span] = block.astype(BF16)
        copy = pltpu.make_async_copy(scratch.at[:, span], out.at[:, pl.ds(low, block.shape[1])], sems.at[index])
        copy.start()
        copies.append(copy)
        start += block.shape[1]
    for copy in copies:
        copy.wait()


def remote_kernel(first, other_seq, other_group, terms, mine, other, weight, total, out, scratch, sems):
    block = weight.shape[1]
    low = pl.multiple_of(first + quarter(other_seq, other_group) * block, 128)
    product = jnp.dot(both(mine, other), weight[...], preferred_element_type=F32)
    write_blocks([(terms[:, pl.ds(low, block)].astype(F32) + product, low)], out, scratch, sems)


def add_kernel(low, terms, came, total, out, scratch, sems):
    blocks, start = [], 0
    for columns in unshared_columns(low, came.shape[1] - low):
        block = terms[:, columns].astype(F32) + came[:, pl.ds(start, columns.size)].astype(F32)
        blocks.append((block, columns.start))
        start += columns.size
    write_blocks(blocks, out, scratch, sems)


def finish_block(kernel, name, operands, total, rows, width, block):
    count = len(operands)
    if total is None:
        body = lambda *refs: kernel(*refs[:count], None, *refs[count:])
        totals, aliases = [], {}
    else:
        body, totals, aliases = kernel, [in_hbm(total)], {count: 0}
    return pl.pallas_call(
        body,
        in_specs=[VMEM] * count + [HBM] * len(totals),
        out_specs=HBM,
        out_shape=pltpu.HBM((rows, width), BF16),
        input_output_aliases=aliases,
        scratch_shapes=[pltpu.VMEM((rows, block), BF16), pltpu.SemaphoreType.DMA((2,))],
        compiler_params=params(),
        name=name,
        cost_estimate=SHORT,
    )(*map(in_vmem, operands), *totals)


def add_remote(terms, mine, other, weight, first, other_seq, other_group, total):
    kernel = functools.partial(remote_kernel, first, other_seq, other_group)
    return finish_block(kernel, "add_remote", (terms, mine, other, weight), total, *terms.shape, weight.shape[1])


def add_unshared(terms, came, low, total):
    kernel = functools.partial(add_kernel, low)
    return finish_block(kernel, "add_unshared", (terms, came), total, *terms.shape, came.shape[1])


def local(queries, cur_keys, cur_values, mem_keys, mem_values, frame_ids, frame_counts, out_weight):
    seq_count = lax.axis_size("seq")
    heads = queries.shape[1] // HD // 2
    keys = cur_keys.shape[0]
    out_cols = out_weight.shape[1]
    share = out_cols // 5 // 128 * 128
    low = out_cols - 4 * share

    *sends, to_sibling = pack(frame_ids, mem_keys, mem_values, cur_keys, cur_values, seq_count)
    columns = pack_columns(out_weight, low, share, to_sibling)
    mine = [sends[0]]
    for shift in range(1, seq_count):
        pairs = [(index, (index + shift) % seq_count) for index in range(seq_count)]
        mine.append(lax.ppermute(sends[shift], "seq", pairs))
    columns = lax.ppermute(columns, "head", SWAP)
    sibling = lax.ppermute(to_sibling, "sub", SWAP)

    held, lse, q = attend_current(queries, cur_keys, cur_values, sibling, heads)
    weight, bias = load(frame_ids, frame_counts, out_weight, seq_count, lse)
    passed = pass_on(mine[1:], weight)
    theirs = lax.ppermute(passed, "sub", SWAP)
    others = [sibling] + [theirs] * (seq_count - 1)
    starts = [2 * keys] + [2 * FT * index for index in range(seq_count - 1)]

    state = attend_frames("far_first", far_half, bias, 0, q, held, lse, mine, [0] * seq_count, False, (passed,))
    far = attend_frames("far_last", far_half, bias, seq_count, q, *state, others, starts, True)
    came_mine = lax.ppermute(far, "head", SWAP)
    far_sibling = lax.ppermute(far, "sub", SWAP)
    group_columns = lax.ppermute(columns, "groups", SWAP)
    columns_copy = copied(columns, far)
    seq_columns = lax.ppermute(columns_copy, "seq", [(index, index ^ 1) for index in range(seq_count)])
    starts = [0] * seq_count + starts
    near = attend_frames("near", near_half, bias, 0, q, held, lse, mine + others, starts, True, (columns_copy,))
    near_sibling = lax.ppermute(near, "sub", SWAP)

    term = project_unshared(far, far_sibling, weight, low, share, (near,))
    came = lax.ppermute(term, "head", SWAP)
    came_mine = gate(came_mine, term)
    came_other = lax.ppermute(came_mine, "sub", SWAP)
    terms = project(near, near_sibling, weight, (came_mine,))

    arrived = (terms, came_mine, came_other)
    total = add_remote(*arrived, columns, low, False, False, None)
    total = add_remote(*arrived, group_columns, low, False, True, total)
    total = add_remote(*arrived, seq_columns, low, True, False, total)
    return add_unshared(terms, came, low, total)


def local_any(queries, cur_keys, cur_values, mem_keys, mem_values, frame_ids, frame_counts, out_weight):
    seq_count = lax.axis_size("seq")
    sub_count = lax.axis_size("sub")
    seq_index = lax.axis_index("seq")
    owner_self = seq_index * sub_count + lax.axis_index("sub")
    row_count, col_count = queries.shape
    heads = col_count // HD
    mine = row_count // sub_count
    wanted = jnp.sum(jnp.where(frame_ids // FR_DEV == owner_self, frame_ids, 0), axis=1) - owner_self * FR_DEV
    own_list = lax.dynamic_index_in_dim(frame_ids, seq_index, 0, keepdims=False)
    owners = jnp.arange(seq_count * sub_count, dtype=jnp.int32)
    hit = (own_list // FR_DEV)[None, :] == owners[:, None]
    got_ids = jnp.sum(jnp.where(hit, own_list[None, :], 0), axis=1).reshape(seq_count, sub_count).T.reshape(-1)
    live = jnp.arange(FT, dtype=jnp.int32)[None, :] < jnp.take(frame_counts, got_ids)[:, None]

    def spread(cached, current):
        sent = lax.all_to_all(jnp.take(cached, wanted, axis=0), "seq", split_axis=0, concat_axis=0, tiled=True)
        far = lax.all_gather(sent, "sub").reshape(-1, heads, HD)
        return jnp.concatenate([lax.all_gather(current, "sub").reshape(-1, heads, HD), far], axis=0)

    keys, values = spread(mem_keys, cur_keys), spread(mem_values, cur_values)
    key_live = jnp.concatenate([jnp.ones((keys.shape[0] - live.size,), bool), live.reshape(-1)])
    start = lax.axis_index("sub") * mine
    query_heads = lax.dynamic_slice_in_dim(queries, start, mine, 0).reshape(mine, heads, HD)
    scores = jnp.einsum("qhd,khd->hqk", query_heads, keys, preferred_element_type=F32) / math.sqrt(HD)
    scores = jnp.where(key_live[None, None, :], scores, -jnp.inf)
    expo = jnp.exp(scores - jnp.max(scores, axis=-1, keepdims=True))
    total = jnp.sum(expo, axis=-1)
    weighted = jnp.einsum("hqk,khd->qhd", expo.astype(BF16), values, preferred_element_type=F32)
    attended = (weighted / total.T[:, :, None]).reshape(mine, col_count).astype(BF16)
    attended = lax.all_gather(attended, "sub", axis=0, tiled=True)
    term = jnp.dot(attended, out_weight, preferred_element_type=F32).astype(BF16)
    return lax.psum_scatter(term, "head", scatter_dimension=0, tiled=True)


def solution(mesh):
    in_specs = (
        P(("groups", "seq"), "head"),
        P(("groups", "seq", "sub"), "head"),
        P(("groups", "seq", "sub"), "head"),
        P(("groups", "seq", "sub"), None, "head"),
        P(("groups", "seq", "sub"), None, "head"),
        P("groups", None),
        P("groups"),
        P("head", "sub"),
    )
    out_specs = P(("groups", "seq", "head"), "sub")

    def apply(queries, *rest):
        heads = queries.shape[1] // mesh.shape["head"] // HD
        paired = heads % 2 == 0 and mesh.shape["seq"] % 2 == 0
        paired = paired and all(mesh.shape[axis] == 2 for axis in ("groups", "head", "sub"))
        body = local if paired else local_any
        return jax.shard_map(body, mesh=mesh, in_specs=in_specs, out_specs=out_specs, check_vma=False)(queries, *rest)

    return apply
```

profile of v0, /device:TPU:0, one launch (start us, length us, event | category | flops | bytes accessed | tf_op | source)
XLA Modules:
  0.0 79.3 jit_solution(13765274451314634826)
XLA Ops:
  0.0 2.7 %pack.1 = (bf16[128,640]{1,0:T(8,128)(2,1)S(1)}, bf16[256,640]{1,0:T(8,128)(2,1)S(1)}, bf16[256,640]{1,0:T(8,128)(2,1)S(1)}, bf16[256,640]{1,0:T(8,128)(2,1)S(1)}, bf16[1152,640]{1,0:T(8,128)(2,1)S(1)}) custom-call(s32[4,8]{1,0:T(4,128)} %ids.3, bf16[16,64,1280]{2,1,0:T(8,128)(2,1)} %keys.1, bf16[16,64,1280]{2,1,0:T(8,128)(2,1)} %values.1, ...), custom_call_target="tpu_custom_call" | custom-call | bytes 12582912 | tf_op jit(solution)/shard_map/pack/pallas_call | solution.py:98
  3.2 2.6 %collective-permute-start.1 = (bf16[256,640]{1,0:T(8,128)(2,1)S(1)}, bf16[256,640]{1,0:T(8,128)(2,1)S(1)}, u32[]{:S(2)}, u32[]{:S(2)}) collective-permute-start(bf16[256,640]{1,0:T(8,128)(2,1)S(1)} %get-tuple-element.23), channel_id=1, source_target_pairs={{0,4},{4,8},{8,12},{12,0},{1,5},{5,9},{9,13},{13,1},{2,6},{6,10},{... | collective-permute-start | bytes 983048 | tf_op jit(solution)/shard_map/ppermute | solution.py:463
  5.9 2.6 %collective-permute-start.2 = (bf16[256,640]{1,0:T(8,128)(2,1)S(1)}, bf16[256,640]{1,0:T(8,128)(2,1)S(1)}, u32[]{:S(2)}, u32[]{:S(2)}) collective-permute-start(bf16[256,640]{1,0:T(8,128)(2,1)S(1)} %get-tuple-element.24), channel_id=1, source_target_pairs={{0,8},{4,12},{8,0},{12,4},{1,9},{5,13},{9,1},{13,5},{2,10},{6,14},... | collective-permute-start | bytes 983048 | tf_op jit(solution)/shard_map/ppermute | solution.py:463
  8.5 1.3 %collective-permute-start.3 = (bf16[256,640]{1,0:T(8,128)(2,1)S(1)}, bf16[256,640]{1,0:T(8,128)(2,1)S(1)}, u32[]{:S(2)}, u32[]{:S(2)}) collective-permute-start(bf16[256,640]{1,0:T(8,128)(2,1)S(1)} %get-tuple-element.25), channel_id=1, source_target_pairs={{0,12},{4,0},{8,4},{12,8},{1,13},{5,1},{9,5},{13,9},{2,14},{6,2},{... | collective-permute-start | bytes 983048 | tf_op jit(solution)/shard_map/ppermute | solution.py:463
  9.8 1.5 %pack_columns.1 = bf16[1280,512]{1,0:T(8,128)(2,1)S(1)} custom-call(bf16[1280,2560]{1,0:T(8,128)(2,1)} %weight.3, bf16[1152,640]{1,0:T(8,128)(2,1)S(1)} %get-tuple-element.17.after), custom_call_target="tpu_custom_call" | custom-call | flops 1024 | bytes 1024 | tf_op jit(solution)/shard_map/pack_columns/pallas_call | solution.py:119
  11.3 1.6 %collective-permute-start.5 = (bf16[1280,512]{1,0:T(8,128)(2,1)S(1)}, bf16[1280,512]{1,0:T(8,128)(2,1)S(1)}, u32[]{:S(2)}, u32[]{:S(2)}) collective-permute-start(bf16[1280,512]{1,0:T(8,128)(2,1)S(1)} %pack_columns.1), channel_id=1, source_target_pairs={{0,2},{2,0},{1,3},{3,1},{4,6},{6,4},{5,7},{7,5},{8,10},{10,8},{9,1... | collective-permute-start | bytes 3932168 | tf_op jit(solution)/shard_map/ppermute | solution.py:464
  12.8 11.3 %attend_current.1 = (f32[5,1024,128]{2,1,0:T(8,128)S(1)}, f32[5,1024,128]{2,1,0:T(8,128)S(1)}, bf16[1024,640]{1,0:T(8,128)(2,1)S(1)}) custom-call(bf16[1024,1280]{1,0:T(8,128)(2,1)} %queries.1, bf16[512,1280]{1,0:T(8,128)(2,1)} %own_keys.1, bf16[512,1280]{1,0:T(8,128)(2,1)} %own_values.1, bf16[1152,640]{1,0:T(8,128)(2,1)S(1)} %collective-permute-done.sibling.rest_0_.rest_4_), custom_call_target="tpu_custom_call" | custom-call | flops 40265318400 | bytes 7864320 | tf_op jit(solution)/shard_map/attend_current/pallas_call | solution.py:253
  24.1 3.6 %load.1 = (bf16[1280,2560]{1,0:T(8,128)(2,1)S(1)}, f32[8,64]{1,0:T(8,128)S(1)}) custom-call(s32[4,8]{1,0:T(4,128)} %ids.3, s32[128]{0:T(128)} %counts.1, bf16[1280,2560]{1,0:T(8,128)(2,1)} %weight.3, f32[5,1024,128]{2,1,0:T(8,128)S(1)} %get-tuple-element.18.after.lse), custom_call_target="tpu_custom_call" | custom-call | bytes 6553600 | tf_op jit(solution)/shard_map/load/pallas_call | solution.py:172
  27.8 2.6 %collective-permute-done.2.refs_1_.rest_2_ = bf16[256,640]{1,0:T(8,128)(2,1)S(1)} collective-permute-done((bf16[256,640]{1,0:T(8,128)(2,1)S(1)}, bf16[256,640]{1,0:T(8,128)(2,1)S(1)}, u32[]{:S(2)}, u32[]{:S(2)}) %collective-permute-start.2) | collective-permute-done | bytes 327712 | tf_op jit(solution)/shard_map/ppermute | solution.py:463
  30.5 1.4 %far_first.1 = (f32[5,512,128]{2,1,0:T(8,128)S(1)}, f32[5,512,128]{2,1,0:T(8,128)S(1)}) custom-call(f32[8,64]{1,0:T(8,128)S(1)} %get-tuple-element.19.bias, bf16[1024,640]{1,0:T(8,128)(2,1)S(1)} %get-tuple-element.20.q, f32[5,1024,128]{2,1,0:T(8,128)S(1)} %get-tuple-element.21.held, f32[5,1024,128]{2,1,0:T(8,128)S(1)} %get-tuple-element.18.after.lse, ...), custom_call_target="tpu_custom_call" | custom-call | flops 1024 | bytes 1024 | tf_op jit(solution)/shard_map/far_first/pallas_call | solution.py:326
  32.4 1.4 %far_last.1.after.mine = bf16[512,640]{1,0:T(8,128)(2,1)S(1)} custom-call(f32[8,64]{1,0:T(8,128)S(1)} %get-tuple-element.19.bias, bf16[1024,640]{1,0:T(8,128)(2,1)S(1)} %get-tuple-element.20.q, f32[5,512,128]{2,1,0:T(8,128)S(1)} %get-tuple-element.27.held, f32[5,512,128]{2,1,0:T(8,128)S(1)} %get-tuple-element.28.lse, ...), custom_call_target="tpu_custom_call" | custom-call | flops 1024 | bytes 1024 | tf_op jit(solution)/shard_map/far_last/pallas_call | solution.py:326
  33.9 1.5 %collective-permute-start.7 = (bf16[512,640]{1,0:T(8,128)(2,1)S(1)}, bf16[512,640]{1,0:T(8,128)(2,1)S(1)}, u32[]{:S(2)}, u32[]{:S(2)}) collective-permute-start(bf16[512,640]{1,0:T(8,128)(2,1)S(1)} %far_last.1.after.mine), channel_id=1, source_target_pairs={{0,2},{2,0},{1,3},{3,1},{4,6},{6,4},{5,7},{7,5},{8,10},{10,8},{9,1... | collective-permute-start | bytes 1966088 | tf_op jit(solution)/shard_map/ppermute | solution.py:476
  35.4 7.6 %collective-permute-done.5.array.refs_3_ = bf16[1280,512]{1,0:T(8,128)(2,1)S(1)} collective-permute-done((bf16[1280,512]{1,0:T(8,128)(2,1)S(1)}, bf16[1280,512]{1,0:T(8,128)(2,1)S(1)}, u32[]{:S(2)}, u32[]{:S(2)}) %collective-permute-start.5) | collective-permute-done | bytes 1310752 | tf_op jit(solution)/shard_map/ppermute | solution.py:464
  43.0 1.5 %collective-permute-start.12 = (bf16[1280,512]{1,0:T(8,128)(2,1)S(1)}, bf16[1280,512]{1,0:T(8,128)(2,1)S(1)}, u32[]{:S(2)}, u32[]{:S(2)}) collective-permute-start(bf16[1280,512]{1,0:T(8,128)(2,1)S(1)} %collective-permute-done.5.array.refs_3_), channel_id=1, source_target_pairs={{0,16},{16,0},{1,17},{17,1},{2,18},{18,2},{3,19},{19,3},{4,20},{20... | collective-permute-start | bytes 3932168 | tf_op jit(solution)/shard_map/ppermute | solution.py:478
  44.7 2.1 %near.1.rest_0_.mine = bf16[512,640]{1,0:T(8,128)(2,1)S(1)} custom-call(f32[8,64]{1,0:T(8,128)S(1)} %get-tuple-element.19.bias, bf16[1024,640]{1,0:T(8,128)(2,1)S(1)} %get-tuple-element.20.q, f32[5,1024,128]{2,1,0:T(8,128)S(1)} %get-tuple-element.21.held, f32[5,1024,128]{2,1,0:T(8,128)S(1)} %get-tuple-element.18.after.lse, ...), custom_call_target="tpu_custom_call" | custom-call | flops 1024 | bytes 1024 | tf_op jit(solution)/shard_map/near/pallas_call | solution.py:326
  46.8 1.6 %project_unshared.1.refs_1_ = bf16[512,1024]{1,0:T(8,128)(2,1)S(1)} custom-call(bf16[512,640]{1,0:T(8,128)(2,1)S(1)} %far_last.1.after.mine, bf16[512,640]{1,0:T(8,128)(2,1)S(1)} %collective-permute-done.8.other, bf16[1280,2560]{1,0:T(8,128)(2,1)S(1)} %get-tuple-element.26.refs_3_.weight, bf16[512,640]{1,0:T(8,128)(2,1)S(1)} %near.1.rest_0_.mine), custom_call_target="tpu_custom_call" | custom-call | flops 1024 | bytes 1024 | tf_op jit(solution)/shard_map/project_unshared/pallas_call | solution.py:371
  48.4 1.6 %collective-permute-start.9 = (bf16[512,1024]{1,0:T(8,128)(2,1)S(1)}, bf16[512,1024]{1,0:T(8,128)(2,1)S(1)}, u32[]{:S(2)}, u32[]{:S(2)}) collective-permute-start(bf16[512,1024]{1,0:T(8,128)(2,1)S(1)} %project_unshared.1.refs_1_), channel_id=1, source_target_pairs={{0,2},{2,0},{1,3},{3,1},{4,6},{6,4},{5,7},{7,5},{8,10},{10,8},{9,1... | collective-permute-start | bytes 3145736 | tf_op jit(solution)/shard_map/ppermute | solution.py:486
  50.0 7.1 %collective-permute-done.7.refs_0_ = bf16[512,640]{1,0:T(8,128)(2,1)S(1)} collective-permute-done((bf16[512,640]{1,0:T(8,128)(2,1)S(1)}, bf16[512,640]{1,0:T(8,128)(2,1)S(1)}, u32[]{:S(2)}, u32[]{:S(2)}) %collective-permute-start.7) | collective-permute-done | bytes 655392 | tf_op jit(solution)/shard_map/ppermute | solution.py:476
  57.1 4.4 %project.1.refs_0_.terms = bf16[512,2560]{1,0:T(8,128)(2,1)S(1)} custom-call(bf16[512,640]{1,0:T(8,128)(2,1)S(1)} %near.1.rest_0_.mine, bf16[512,640]{1,0:T(8,128)(2,1)S(1)} %collective-permute-done.6.other, bf16[1280,2560]{1,0:T(8,128)(2,1)S(1)} %get-tuple-element.26.refs_3_.weight, bf16[512,640]{1,0:T(8,128)(2,1)S(1)} %gate.1.rest_0_.refs_1_.mine), custom_call_target="tpu_custom_call" | custom-call | flops 1024 | bytes 1024 | tf_op jit(solution)/shard_map/project/pallas_call | solution.py:371
  61.5 1.7 %add_remote.3.total = bf16[512,2560]{1,0:T(8,128)(2,1)} custom-call(bf16[512,2560]{1,0:T(8,128)(2,1)S(1)} %project.1.refs_0_.terms, bf16[512,640]{1,0:T(8,128)(2,1)S(1)} %gate.1.rest_0_.refs_1_.mine, bf16[512,640]{1,0:T(8,128)(2,1)S(1)} %collective-permute-done.10.refs_2_.other, bf16[1280,512]{1,0:T(8,128)(2,1)S(1)} %collective-permute-done.5.array.refs_3_), custom_call_target="tpu_custom_call" | custom-call | flops 1024 | bytes 1024 | tf_op jit(solution)/shard_map/add_remote/pallas_call | solution.py:427
  63.2 7.8 %collective-permute-done.12.weight = bf16[1280,512]{1,0:T(8,128)(2,1)S(1)} collective-permute-done((bf16[1280,512]{1,0:T(8,128)(2,1)S(1)}, bf16[1280,512]{1,0:T(8,128)(2,1)S(1)}, u32[]{:S(2)}, u32[]{:S(2)}) %collective-permute-start.12) | collective-permute-done | bytes 1310752 | tf_op jit(solution)/shard_map/ppermute | solution.py:478
  71.0 1.7 %add_remote.4.total = bf16[512,2560]{1,0:T(8,128)(2,1)} custom-call(bf16[512,2560]{1,0:T(8,128)(2,1)S(1)} %project.1.refs_0_.terms, bf16[512,640]{1,0:T(8,128)(2,1)S(1)} %gate.1.rest_0_.refs_1_.mine, bf16[512,640]{1,0:T(8,128)(2,1)S(1)} %collective-permute-done.10.refs_2_.other, ...), custom_call_target="tpu_custom_call", output_to_operand_aliasing={{}: (4, {})} | custom-call | flops 1024 | bytes 1024 | tf_op jit(solution)/shard_map/add_remote/pallas_call | solution.py:427
  73.4 1.7 %add_remote.5.total = bf16[512,2560]{1,0:T(8,128)(2,1)} custom-call(bf16[512,2560]{1,0:T(8,128)(2,1)S(1)} %project.1.refs_0_.terms, bf16[512,640]{1,0:T(8,128)(2,1)S(1)} %gate.1.rest_0_.refs_1_.mine, bf16[512,640]{1,0:T(8,128)(2,1)S(1)} %collective-permute-done.10.refs_2_.other, ...), custom_call_target="tpu_custom_call", output_to_operand_aliasing={{}: (4, {})} | custom-call | flops 1024 | bytes 1024 | tf_op jit(solution)/shard_map/add_remote/pallas_call | solution.py:427
  75.1 3.1 %collective-permute-done.9.came = bf16[512,1024]{1,0:T(8,128)(2,1)S(1)} collective-permute-done((bf16[512,1024]{1,0:T(8,128)(2,1)S(1)}, bf16[512,1024]{1,0:T(8,128)(2,1)S(1)}, u32[]{:S(2)}, u32[]{:S(2)}) %collective-permute-start.9) | collective-permute-done | bytes 1048608 | tf_op jit(solution)/shard_map/ppermute | solution.py:486
  (18 shorter events, 3.2 us)
Async XLA Ops:
  2.7 10.1 %collective-permute-start = (bf16[1152,640]{1,0:T(8,128)(2,1)S(1)}, bf16[1152,640]{1,0:T(8,128)(2,1)S(1)}, u32[]{:S(2)}, u32[]{:S(2)}) collective-permute-start(bf16[1152,640]{1,0:T(8,128)(2,1)S(1)} %get-tuple-element.17.after), channel_id=1, source_target_pairs={{0,1},{1,0},{2,3},{3,2},{4,5},{5,4},{6,7},{7,6},{8,9},{9,8},{10,11... | collective-permute-start | bytes 4423688 | tf_op jit(solution)/shard_map/ppermute | solution.py:465
  3.2 24.6 %collective-permute-start.1 = (bf16[256,640]{1,0:T(8,128)(2,1)S(1)}, bf16[256,640]{1,0:T(8,128)(2,1)S(1)}, u32[]{:S(2)}, u32[]{:S(2)}) collective-permute-start(bf16[256,640]{1,0:T(8,128)(2,1)S(1)} %get-tuple-element.23), channel_id=1, source_target_pairs={{0,4},{4,8},{8,12},{12,0},{1,5},{5,9},{9,13},{13,1},{2,6},{6,10},{... | collective-permute-start | bytes 983048 | tf_op jit(solution)/shard_map/ppermute | solution.py:463
  5.9 24.5 %collective-permute-start.2 = (bf16[256,640]{1,0:T(8,128)(2,1)S(1)}, bf16[256,640]{1,0:T(8,128)(2,1)S(1)}, u32[]{:S(2)}, u32[]{:S(2)}) collective-permute-start(bf16[256,640]{1,0:T(8,128)(2,1)S(1)} %get-tuple-element.24), channel_id=1, source_target_pairs={{0,8},{4,12},{8,0},{12,4},{1,9},{5,13},{9,1},{13,5},{2,10},{6,14},... | collective-permute-start | bytes 983048 | tf_op jit(solution)/shard_map/ppermute | solution.py:463
  8.5 21.9 %collective-permute-start.3 = (bf16[256,640]{1,0:T(8,128)(2,1)S(1)}, bf16[256,640]{1,0:T(8,128)(2,1)S(1)}, u32[]{:S(2)}, u32[]{:S(2)}) collective-permute-start(bf16[256,640]{1,0:T(8,128)(2,1)S(1)} %get-tuple-element.25), channel_id=1, source_target_pairs={{0,12},{4,0},{8,4},{12,8},{1,13},{5,1},{9,5},{13,9},{2,14},{6,2},{... | collective-permute-start | bytes 983048 | tf_op jit(solution)/shard_map/ppermute | solution.py:463
  11.3 31.8 %collective-permute-start.5 = (bf16[1280,512]{1,0:T(8,128)(2,1)S(1)}, bf16[1280,512]{1,0:T(8,128)(2,1)S(1)}, u32[]{:S(2)}, u32[]{:S(2)}) collective-permute-start(bf16[1280,512]{1,0:T(8,128)(2,1)S(1)} %pack_columns.1), channel_id=1, source_target_pairs={{0,2},{2,0},{1,3},{3,1},{4,6},{6,4},{5,7},{7,5},{8,10},{10,8},{9,1... | collective-permute-start | bytes 3932168 | tf_op jit(solution)/shard_map/ppermute | solution.py:464
  30.4 1.9 %collective-permute-start.4 = (bf16[384,640]{1,0:T(8,128)(2,1)S(1)}, bf16[384,640]{1,0:T(8,128)(2,1)S(1)}, u32[]{:S(2)}, u32[]{:S(2)}) collective-permute-start(bf16[384,640]{1,0:T(8,128)(2,1)S(1)} %pass_on.1.rest_4_), channel_id=1, source_target_pairs={{0,1},{1,0},{2,3},{3,2},{4,5},{5,4},{6,7},{7,6},{8,9},{9,8},{10,11... | collective-permute-start | bytes 1474568 | tf_op jit(solution)/shard_map/ppermute | solution.py:470
  33.7 13.1 %collective-permute-start.8 = (bf16[512,640]{1,0:T(8,128)(2,1)S(1)}, bf16[512,640]{1,0:T(8,128)(2,1)S(1)}, u32[]{:S(2)}, u32[]{:S(2)}) collective-permute-start(bf16[512,640]{1,0:T(8,128)(2,1)S(1)} %far_last.1.after.mine), channel_id=1, source_target_pairs={{0,1},{1,0},{2,3},{3,2},{4,5},{5,4},{6,7},{7,6},{8,9},{9,8},{10,11... | collective-permute-start | bytes 1966088 | tf_op jit(solution)/shard_map/ppermute | solution.py:477
  33.9 23.2 %collective-permute-start.7 = (bf16[512,640]{1,0:T(8,128)(2,1)S(1)}, bf16[512,640]{1,0:T(8,128)(2,1)S(1)}, u32[]{:S(2)}, u32[]{:S(2)}) collective-permute-start(bf16[512,640]{1,0:T(8,128)(2,1)S(1)} %far_last.1.after.mine), channel_id=1, source_target_pairs={{0,2},{2,0},{1,3},{3,1},{4,6},{6,4},{5,7},{7,5},{8,10},{10,8},{9,1... | collective-permute-start | bytes 1966088 | tf_op jit(solution)/shard_map/ppermute | solution.py:476
  43.0 28.0 %collective-permute-start.12 = (bf16[1280,512]{1,0:T(8,128)(2,1)S(1)}, bf16[1280,512]{1,0:T(8,128)(2,1)S(1)}, u32[]{:S(2)}, u32[]{:S(2)}) collective-permute-start(bf16[1280,512]{1,0:T(8,128)(2,1)S(1)} %collective-permute-done.5.array.refs_3_), channel_id=1, source_target_pairs={{0,16},{16,0},{1,17},{17,1},{2,18},{18,2},{3,19},{19,3},{4,20},{20... | collective-permute-start | bytes 3932168 | tf_op jit(solution)/shard_map/ppermute | solution.py:478
  44.7 28.7 %collective-permute-start.11 = (bf16[1280,512]{1,0:T(8,128)(2,1)S(1)}, bf16[1280,512]{1,0:T(8,128)(2,1)S(1)}, u32[]{:S(2)}, u32[]{:S(2)}) collective-permute-start(bf16[1280,512]{1,0:T(8,128)(2,1)S(1)} %copied.1.rest_8_), channel_id=1, source_target_pairs={{0,4},{4,0},{8,12},{12,8},{1,5},{5,1},{9,13},{13,9},{2,6},{6,2},{1... | collective-permute-start | bytes 3932168 | tf_op jit(solution)/shard_map/ppermute | solution.py:480
  48.4 29.8 %collective-permute-start.9 = (bf16[512,1024]{1,0:T(8,128)(2,1)S(1)}, bf16[512,1024]{1,0:T(8,128)(2,1)S(1)}, u32[]{:S(2)}, u32[]{:S(2)}) collective-permute-start(bf16[512,1024]{1,0:T(8,128)(2,1)S(1)} %project_unshared.1.refs_1_), channel_id=1, source_target_pairs={{0,2},{2,0},{1,3},{3,1},{4,6},{6,4},{5,7},{7,5},{8,10},{10,8},{9,1... | collective-permute-start | bytes 3145736 | tf_op jit(solution)/shard_map/ppermute | solution.py:486
  50.0 7.1 %collective-permute-start.6 = (bf16[512,640]{1,0:T(8,128)(2,1)S(1)}, bf16[512,640]{1,0:T(8,128)(2,1)S(1)}, u32[]{:S(2)}, u32[]{:S(2)}) collective-permute-start(bf16[512,640]{1,0:T(8,128)(2,1)S(1)} %near.1.rest_0_.mine), channel_id=1, source_target_pairs={{0,1},{1,0},{2,3},{3,2},{4,5},{5,4},{6,7},{7,6},{8,9},{9,8},{10,11... | collective-permute-start | bytes 1966088 | tf_op jit(solution)/shard_map/ppermute | solution.py:483
  57.1 4.4 %collective-permute-start.10 = (bf16[512,640]{1,0:T(8,128)(2,1)S(1)}, bf16[512,640]{1,0:T(8,128)(2,1)S(1)}, u32[]{:S(2)}, u32[]{:S(2)}) collective-permute-start(bf16[512,640]{1,0:T(8,128)(2,1)S(1)} %gate.1.rest_0_.refs_1_.mine), channel_id=1, source_target_pairs={{0,1},{1,0},{2,3},{3,2},{4,5},{5,4},{6,7},{7,6},{8,9},{9,8},{10,11... | collective-permute-start | bytes 1966088 | tf_op jit(solution)/shard_map/ppermute | solution.py:488
where the time goes:
time: 79.5 us; the launch traced here: 79.3 us
  Pallas kernels  36.2 us (46%)
  waiting for transfers between devices  29.3 us (37%)
  starting transfers between devices  13.6 us (17%)
    pallas_call x1, Pallas kernels, attend_current(): pl.pallas_call(functools.partial(current_kernel, 512), in_specs=[HBM] * 3...  11.3 us
    ppermute x1, waiting for transfers between devices, local(): group_columns = lax.ppermute(columns, 'groups', SWAP)  7.83 us
    ppermute x1, waiting for transfers between devices, local(): columns = lax.ppermute(columns, 'head', SWAP)  7.6 us
    ppermute x1, waiting for transfers between devices, local(): came_mine = lax.ppermute(far, 'head', SWAP)  7.13 us
    ppermute x3, starting transfers between devices, local(): mine.append(lax.ppermute(sends[shift], 'seq', pairs))  6.57 us
    pallas_call x4, Pallas kernels, finish_block(): pl.pallas_call(body, in_specs=[VMEM] * count + [HBM] * len(totals), out_s...  6.15 us
    pallas_call x2, Pallas kernels, project_call(): pl.pallas_call(kernel, in_specs=[VMEM] * 3 + [ANY] * len(after), out_spec...  5.93 us
    pallas_call x3, Pallas kernels, attend_frames(): pl.pallas_call(functools.partial(frames_kernel, heads, half, state_half,...  4.9 us
  transfers between devices with their start and end apart: 13, of which 7 were waited for; matrix products, arithmetic and copies ran while one was open for 0% of the time, Pallas kernels for 41%

commit v1 on v0

--- a/solution.py
+++ b/solution.py
@@ -58,22 +58,42 @@
     return found
 
 
-def pack_kernel(seq_count, parts, ids, keys, values, cur_keys, cur_values, *rest):
+def pack_kernel(seq_count, low, parts, ids_in, keys, values, cur_keys, cur_values, weight, *rest):
     outs = rest[:seq_count]
-    sibling, sems = rest[seq_count:]
+    sibling, columns_out, ids, sems = rest[seq_count:]
     seq_index = lax.axis_index("seq")
     sub_index = lax.axis_index("sub")
     width = sibling.shape[1]
+    block = columns_out.shape[1]
     count = cur_keys.shape[0]
     frame_count = 2 * seq_count
+    copies = []
+
+    def start(source, target):
+        copy = pltpu.make_async_copy(source, target, sems.at[len(copies)])
+        copy.start()
+        copies.append(copy)
+        return copy
 
     def columns_of(half):
         return pl.ds(pl.multiple_of(half * width, 128), width)
 
-    pairs = []
+    listed = start(ids_in, ids)
+    rows = count // parts
+    for part, source in enumerate((cur_keys, cur_values)):
+        for low_row in range(0, count, rows):
+            target = sibling.at[pl.ds(part * count + low_row, rows), :]
+            start(source.at[pl.ds(low_row, rows), columns_of(1 - sub_index)], target)
+    first = pl.multiple_of(low + quarter(False, False) * block, 128)
+    rows = weight.shape[0] // parts
+    for part in range(parts):
+        span = pl.ds(part * rows, rows)
+        start(weight.at[span, pl.ds(first, block)], columns_out.at[span, :])
+    listed.wait()
     for shift, out in enumerate(outs):
         owner = seq_index * 2 + sub_index
         wanted = held_by(ids, lax.rem(seq_index + shift, seq_count), owner, frame_count) - owner * FR_DEV
+        wanted = jnp.clip(wanted, 0, FR_DEV - 1)
         for turn in range(2):
             half = sub_index if turn == 0 else 1 - sub_index
             for part, source in enumerate((keys, values)):
@@ -81,51 +101,29 @@
                     target = sibling.at[pl.ds(2 * count + part * FT, FT), :]
                 else:
                     target = out.at[pl.ds((2 * turn + part) * FT, FT), :]
-                pairs.append((source.at[wanted, :, columns_of(half)], target))
-    rows = count // parts
-    for part, source in enumerate((cur_keys, cur_values)):
-        for low_row in range(0, count, rows):
-            target = sibling.at[pl.ds(part * count + low_row, rows), :]
-            pairs.append((source.at[pl.ds(low_row, rows), columns_of(1 - sub_index)], target))
-    copy_all(pairs, sems)
-
-
-def pack(frame_ids, mem_keys, mem_values, cur_keys, cur_values, seq_count):
+                start(source.at[wanted, :, columns_of(half)], target)
+    for copy in copies[1:]:
+        copy.wait()
+
+
+def pack(frame_ids, mem_keys, mem_values, cur_keys, cur_values, weight, low, share, seq_count):
     parts = 4
     width = mem_keys.shape[2] // 2
     rows = [2 * FT] + [4 * FT] * (seq_count - 1) + [2 * cur_keys.shape[0] + 2 * FT]
-    shapes = [(count, width) for count in rows]
-    return pl.pallas_call(
-        functools.partial(pack_kernel, seq_count, parts),
+    shapes = [(count, width) for count in rows] + [(weight.shape[0], share)]
+    return pl.pallas_call(
+        functools.partial(pack_kernel, seq_count, low, parts),
         out_shape=[pltpu.VMEM(shape, BF16) for shape in shapes],
-        in_specs=[pl.BlockSpec(memory_space=pltpu.SMEM)] + [HBM] * 4,
+        in_specs=[HBM] * 6,
         out_specs=[VMEM] * len(shapes),
-        scratch_shapes=[pltpu.SemaphoreType.DMA((4 * seq_count + 2 * parts,))],
+        scratch_shapes=[
+            pltpu.SMEM(frame_ids.shape, jnp.int32),
+            pltpu.SemaphoreType.DMA((1 + 4 * seq_count + 3 * parts,)),
+        ],
         compiler_params=params(),
         name="pack",
         cost_estimate=pl.CostEstimate(flops=0, bytes_accessed=12 * 2**20, transcendentals=0),
-    )(*map(in_hbm, (frame_ids, mem_keys, mem_values, cur_keys, cur_values)))
-
-
-def pack_columns_kernel(low, parts, weight, after, out, sems):
-    first = pl.multiple_of(low + quarter(False, False) * out.shape[1], 128)
-    rows = weight.shape[0] // parts
-    spans = [pl.ds(part * rows, rows) for part in range(parts)]
-    copy_all([(weight.at[span, pl.ds(first, out.shape[1])], out.at[span, :]) for span in spans], sems)
-
-
-def pack_columns(weight, low, share, after):
-    parts = 8
-    return pl.pallas_call(
-        functools.partial(pack_columns_kernel, low, parts),
-        out_shape=pltpu.VMEM((weight.shape[0], share), BF16),
-        in_specs=[HBM, ANY],
-        out_specs=VMEM,
-        scratch_shapes=[pltpu.SemaphoreType.DMA((parts,))],
-        compiler_params=params(),
-        name="pack_columns",
-        cost_estimate=SHORT,
-    )(in_hbm(weight), in_vmem(after))
+    )(*map(in_hbm, (frame_ids, mem_keys, mem_values, cur_keys, cur_values, weight)))
 
 
 def pass_on_kernel(*refs):
@@ -455,8 +453,9 @@
     share = out_cols // 5 // 128 * 128
     low = out_cols - 4 * share
 
-    *sends, to_sibling = pack(frame_ids, mem_keys, mem_values, cur_keys, cur_values, seq_count)
-    columns = pack_columns(out_weight, low, share, to_sibling)
+    *sends, to_sibling, columns = pack(
+        frame_ids, mem_keys, mem_values, cur_keys, cur_values, out_weight, low, share, seq_count
+    )
     mine = [sends[0]]
     for shift in range(1, seq_count):
         pairs = [(index, (index + shift) % seq_count) for index in range(seq_count)]

time: 79.5 us -> 79.2 us (level); the launches traced: 79.3 us -> 77.6 us
  Pallas kernels: 36.2 us -> 34.7 us
    ppermute x1, waiting for transfers between devices: 0.67 us -> 2.25 us  [local(): lax.ppermute(columns_copy, 'seq', [(index, index ^ 1) for index in range(...]
    ppermute x1, waiting for transfers between devices: 3.08 us -> 1.5 us  [local(): came = lax.ppermute(term, 'head', SWAP)]
    ppermute x1, waiting for transfers between devices: 7.6 us -> 6.02 us  [local(): columns = lax.ppermute(columns, 'head', SWAP)]
    pallas_call x2 -> x1, Pallas kernels: 4.17 us -> 2.61 us  [pack(): pl.pallas_call(functools.partial(pack_kernel, seq_count, low, parts), out...]
    ppermute x3, waiting for transfers between devices: 2.58 us -> 4.12 us  [local(): mine.append(lax.ppermute(sends[shift], 'seq', pairs))]
    ppermute x1, starting transfers between devices: 0.07 us -> 1.56 us  [local(): lax.ppermute(columns_copy, 'seq', [(index, index ^ 1) for index in range(...]
    ppermute x1, starting transfers between devices: 1.55 us -> 0.61 us  [local(): came = lax.ppermute(term, 'head', SWAP)]
  transfers between devices with their start and end apart: 13 -> 13, of which waited for: 7 -> 7; matrix products, arithmetic and copies ran while one was open for 0% -> 0% of each run, Pallas kernels for 41% -> 40%
where the time goes in v1:
time: 79.2 us; the launch traced here: 77.6 us
  Pallas kernels  34.7 us (44%)
  waiting for transfers between devices  28.8 us (36%)
  starting transfers between devices  14 us (18%)
    pallas_call x1, Pallas kernels, attend_current(): pl.pallas_call(functools.partial(current_kernel, 512), in_specs=[HBM] * 3...  11.3 us
    ppermute x1, waiting for transfers between devices, local(): group_columns = lax.ppermute(columns, 'groups', SWAP)  7.83 us
    ppermute x1, waiting for transfers between devices, local(): came_mine = lax.ppermute(far, 'head', SWAP)  6.61 us
    ppermute x3, starting transfers between devices, local(): mine.append(lax.ppermute(sends[shift], 'seq', pairs))  6.57 us
    pallas_call x4, Pallas kernels, finish_block(): pl.pallas_call(body, in_specs=[VMEM] * count + [HBM] * len(totals), out_s...  6.15 us
    ppermute x1, waiting for transfers between devices, local(): columns = lax.ppermute(columns, 'head', SWAP)  6.02 us
    pallas_call x2, Pallas kernels, project_call(): pl.pallas_call(kernel, in_specs=[VMEM] * 3 + [ANY] * len(after), out_spec...  5.93 us
    pallas_call x3, Pallas kernels, attend_frames(): pl.pallas_call(functools.partial(frames_kernel, heads, half, state_half,...  4.93 us
  transfers between devices with their start and end apart: 13, of which 7 were waited for; matrix products, arithmetic and copies ran while one was open for 0% of the time, Pallas kernels for 40%

profile of v1, /device:TPU:0, one launch (start us, length us, event | category | flops | bytes accessed | tf_op | source)
XLA Modules:
  0.0 77.6 jit_solution(1438572252534090619)
XLA Ops:
  0.0 2.6 %pack.1 = (bf16[128,640]{1,0:T(8,128)(2,1)S(1)}, bf16[256,640]{1,0:T(8,128)(2,1)S(1)}, bf16[256,640]{1,0:T(8,128)(2,1)S(1)}, bf16[256,640]{1,0:T(8,128)(2,1)S(1)...) custom-call(s32[4,8]{1,0:T(4,128)} %ids.1, bf16[16,64,1280]{2,1,0:T(8,128)(2,1)} %keys.1, ...), custom_call_target="tpu_custom_call" | custom-call | bytes 12582912 | tf_op jit(solution)/shard_map/pack/pallas_call | solution.py:114
  3.1 2.6 %collective-permute-start.1 = (bf16[256,640]{1,0:T(8,128)(2,1)S(1)}, bf16[256,640]{1,0:T(8,128)(2,1)S(1)}, u32[]{:S(2)}, u32[]{:S(2)}) collective-permute-start(bf16[256,640]{1,0:T(8,128)(2,1)S(1)} %get-tuple-element.24), channel_id=1, source_target_pairs={{0,4},{4,8},{8,12},{12,0},{1,5},{5,9},{9,13},{13,1},{2,6},{6,10},{... | collective-permute-start | bytes 983048 | tf_op jit(solution)/shard_map/ppermute | solution.py:462
  5.8 2.6 %collective-permute-start.2 = (bf16[256,640]{1,0:T(8,128)(2,1)S(1)}, bf16[256,640]{1,0:T(8,128)(2,1)S(1)}, u32[]{:S(2)}, u32[]{:S(2)}) collective-permute-start(bf16[256,640]{1,0:T(8,128)(2,1)S(1)} %get-tuple-element.25), channel_id=1, source_target_pairs={{0,8},{4,12},{8,0},{12,4},{1,9},{5,13},{9,1},{13,5},{2,10},{6,14},... | collective-permute-start | bytes 983048 | tf_op jit(solution)/shard_map/ppermute | solution.py:462
  8.4 1.3 %collective-permute-start.3 = (bf16[256,640]{1,0:T(8,128)(2,1)S(1)}, bf16[256,640]{1,0:T(8,128)(2,1)S(1)}, u32[]{:S(2)}, u32[]{:S(2)}) collective-permute-start(bf16[256,640]{1,0:T(8,128)(2,1)S(1)} %get-tuple-element.26), channel_id=1, source_target_pairs={{0,12},{4,0},{8,4},{12,8},{1,13},{5,1},{9,5},{13,9},{2,14},{6,2},{... | collective-permute-start | bytes 983048 | tf_op jit(solution)/shard_map/ppermute | solution.py:462
  9.7 1.5 %collective-permute-start.5 = (bf16[1280,512]{1,0:T(8,128)(2,1)S(1)}, bf16[1280,512]{1,0:T(8,128)(2,1)S(1)}, u32[]{:S(2)}, u32[]{:S(2)}) collective-permute-start(bf16[1280,512]{1,0:T(8,128)(2,1)S(1)} %get-tuple-element.28), channel_id=1, source_target_pairs={{0,2},{2,0},{1,3},{3,1},{4,6},{6,4},{5,7},{7,5},{8,10},{10,8},{9,1... | collective-permute-start | bytes 3932168 | tf_op jit(solution)/shard_map/ppermute | solution.py:463
  11.2 11.3 %attend_current.1 = (f32[5,1024,128]{2,1,0:T(8,128)S(1)}, f32[5,1024,128]{2,1,0:T(8,128)S(1)}, bf16[1024,640]{1,0:T(8,128)(2,1)S(1)}) custom-call(bf16[1024,1280]{1,0:T(8,128)(2,1)} %queries.1, bf16[512,1280]{1,0:T(8,128)(2,1)} %own_keys.1, bf16[512,1280]{1,0:T(8,128)(2,1)} %own_values.1, bf16[1152,640]{1,0:T(8,128)(2,1)S(1)} %collective-permute-done.sibling.rest_0_.rest_4_), custom_call_target="tpu_custom_call" | custom-call | flops 40265318400 | bytes 7864320 | tf_op jit(solution)/shard_map/attend_current/pallas_call | solution.py:251
  22.5 3.6 %load.1 = (bf16[1280,2560]{1,0:T(8,128)(2,1)S(1)}, f32[8,64]{1,0:T(8,128)S(1)}) custom-call(s32[4,8]{1,0:T(4,128)} %ids.1, s32[128]{0:T(128)} %counts.1, bf16[1280,2560]{1,0:T(8,128)(2,1)} %weight.3, f32[5,1024,128]{2,1,0:T(8,128)S(1)} %get-tuple-element.19.after.lse), custom_call_target="tpu_custom_call" | custom-call | bytes 6553600 | tf_op jit(solution)/shard_map/load/pallas_call | solution.py:170
  26.2 4.1 %collective-permute-done.2.refs_1_.rest_2_ = bf16[256,640]{1,0:T(8,128)(2,1)S(1)} collective-permute-done((bf16[256,640]{1,0:T(8,128)(2,1)S(1)}, bf16[256,640]{1,0:T(8,128)(2,1)S(1)}, u32[]{:S(2)}, u32[]{:S(2)}) %collective-permute-start.2) | collective-permute-done | bytes 327712 | tf_op jit(solution)/shard_map/ppermute | solution.py:462
  30.4 1.4 %far_first.1 = (f32[5,512,128]{2,1,0:T(8,128)S(1)}, f32[5,512,128]{2,1,0:T(8,128)S(1)}) custom-call(f32[8,64]{1,0:T(8,128)S(1)} %get-tuple-element.20.bias, bf16[1024,640]{1,0:T(8,128)(2,1)S(1)} %get-tuple-element.21.q, f32[5,1024,128]{2,1,0:T(8,128)S(1)} %get-tuple-element.22.held, f32[5,1024,128]{2,1,0:T(8,128)S(1)} %get-tuple-element.19.after.lse, ...), custom_call_target="tpu_custom_call" | custom-call | flops 1024 | bytes 1024 | tf_op jit(solution)/shard_map/far_first/pallas_call | solution.py:324
  32.3 1.4 %far_last.1.after.mine = bf16[512,640]{1,0:T(8,128)(2,1)S(1)} custom-call(f32[8,64]{1,0:T(8,128)S(1)} %get-tuple-element.20.bias, bf16[1024,640]{1,0:T(8,128)(2,1)S(1)} %get-tuple-element.21.q, f32[5,512,128]{2,1,0:T(8,128)S(1)} %get-tuple-element.29.held, f32[5,512,128]{2,1,0:T(8,128)S(1)} %get-tuple-element.30.lse, ...), custom_call_target="tpu_custom_call" | custom-call | flops 1024 | bytes 1024 | tf_op jit(solution)/shard_map/far_last/pallas_call | solution.py:324
  33.9 1.5 %collective-permute-start.7 = (bf16[512,640]{1,0:T(8,128)(2,1)S(1)}, bf16[512,640]{1,0:T(8,128)(2,1)S(1)}, u32[]{:S(2)}, u32[]{:S(2)}) collective-permute-start(bf16[512,640]{1,0:T(8,128)(2,1)S(1)} %far_last.1.after.mine), channel_id=1, source_target_pairs={{0,2},{2,0},{1,3},{3,1},{4,6},{6,4},{5,7},{7,5},{8,10},{10,8},{9,1... | collective-permute-start | bytes 1966088 | tf_op jit(solution)/shard_map/ppermute | solution.py:475
  35.4 6.0 %collective-permute-done.5.array.refs_3_ = bf16[1280,512]{1,0:T(8,128)(2,1)S(1)} collective-permute-done((bf16[1280,512]{1,0:T(8,128)(2,1)S(1)}, bf16[1280,512]{1,0:T(8,128)(2,1)S(1)}, u32[]{:S(2)}, u32[]{:S(2)}) %collective-permute-start.5) | collective-permute-done | bytes 1310752 | tf_op jit(solution)/shard_map/ppermute | solution.py:463
  41.4 1.5 %collective-permute-start.12 = (bf16[1280,512]{1,0:T(8,128)(2,1)S(1)}, bf16[1280,512]{1,0:T(8,128)(2,1)S(1)}, u32[]{:S(2)}, u32[]{:S(2)}) collective-permute-start(bf16[1280,512]{1,0:T(8,128)(2,1)S(1)} %collective-permute-done.5.array.refs_3_), channel_id=1, source_target_pairs={{0,16},{16,0},{1,17},{17,1},{2,18},{18,2},{3,19},{19,3},{4,20},{20... | collective-permute-start | bytes 3932168 | tf_op jit(solution)/shard_map/ppermute | solution.py:477
  43.0 1.6 %collective-permute-start.11 = (bf16[1280,512]{1,0:T(8,128)(2,1)S(1)}, bf16[1280,512]{1,0:T(8,128)(2,1)S(1)}, u32[]{:S(2)}, u32[]{:S(2)}) collective-permute-start(bf16[1280,512]{1,0:T(8,128)(2,1)S(1)} %copied.1.rest_8_), channel_id=1, source_target_pairs={{0,4},{4,0},{8,12},{12,8},{1,5},{5,1},{9,13},{13,9},{2,6},{6,2},{1... | collective-permute-start | bytes 3932168 | tf_op jit(solution)/shard_map/ppermute | solution.py:479
  44.6 2.1 %near.1.rest_0_.mine = bf16[512,640]{1,0:T(8,128)(2,1)S(1)} custom-call(f32[8,64]{1,0:T(8,128)S(1)} %get-tuple-element.20.bias, bf16[1024,640]{1,0:T(8,128)(2,1)S(1)} %get-tuple-element.21.q, f32[5,1024,128]{2,1,0:T(8,128)S(1)} %get-tuple-element.22.held, f32[5,1024,128]{2,1,0:T(8,128)S(1)} %get-tuple-element.19.after.lse, ...), custom_call_target="tpu_custom_call" | custom-call | flops 1024 | bytes 1024 | tf_op jit(solution)/shard_map/near/pallas_call | solution.py:324
  46.7 1.5 %project_unshared.1.refs_1_ = bf16[512,1024]{1,0:T(8,128)(2,1)S(1)} custom-call(bf16[512,640]{1,0:T(8,128)(2,1)S(1)} %far_last.1.after.mine, bf16[512,640]{1,0:T(8,128)(2,1)S(1)} %collective-permute-done.8.other, bf16[1280,2560]{1,0:T(8,128)(2,1)S(1)} %get-tuple-element.27.refs_3_.weight, bf16[512,640]{1,0:T(8,128)(2,1)S(1)} %near.1.rest_0_.mine), custom_call_target="tpu_custom_call" | custom-call | flops 1024 | bytes 1024 | tf_op jit(solution)/shard_map/project_unshared/pallas_call | solution.py:369
  48.8 6.6 %collective-permute-done.7.refs_0_ = bf16[512,640]{1,0:T(8,128)(2,1)S(1)} collective-permute-done((bf16[512,640]{1,0:T(8,128)(2,1)S(1)}, bf16[512,640]{1,0:T(8,128)(2,1)S(1)}, u32[]{:S(2)}, u32[]{:S(2)}) %collective-permute-start.7) | collective-permute-done | bytes 655392 | tf_op jit(solution)/shard_map/ppermute | solution.py:475
  55.5 4.4 %project.1.refs_0_.terms = bf16[512,2560]{1,0:T(8,128)(2,1)S(1)} custom-call(bf16[512,640]{1,0:T(8,128)(2,1)S(1)} %near.1.rest_0_.mine, bf16[512,640]{1,0:T(8,128)(2,1)S(1)} %collective-permute-done.6.other, bf16[1280,2560]{1,0:T(8,128)(2,1)S(1)} %get-tuple-element.27.refs_3_.weight, bf16[512,640]{1,0:T(8,128)(2,1)S(1)} %gate.1.rest_0_.refs_1_.mine), custom_call_target="tpu_custom_call" | custom-call | flops 1024 | bytes 1024 | tf_op jit(solution)/shard_map/project/pallas_call | solution.py:369
  59.9 1.7 %add_remote.3.total = bf16[512,2560]{1,0:T(8,128)(2,1)} custom-call(bf16[512,2560]{1,0:T(8,128)(2,1)S(1)} %project.1.refs_0_.terms, bf16[512,640]{1,0:T(8,128)(2,1)S(1)} %gate.1.rest_0_.refs_1_.mine, bf16[512,640]{1,0:T(8,128)(2,1)S(1)} %collective-permute-done.10.refs_2_.other, bf16[1280,512]{1,0:T(8,128)(2,1)S(1)} %collective-permute-done.5.array.refs_3_), custom_call_target="tpu_custom_call" | custom-call | flops 1024 | bytes 1024 | tf_op jit(solution)/shard_map/add_remote/pallas_call | solution.py:425
  61.6 7.8 %collective-permute-done.12.weight = bf16[1280,512]{1,0:T(8,128)(2,1)S(1)} collective-permute-done((bf16[1280,512]{1,0:T(8,128)(2,1)S(1)}, bf16[1280,512]{1,0:T(8,128)(2,1)S(1)}, u32[]{:S(2)}, u32[]{:S(2)}) %collective-permute-start.12) | collective-permute-done | bytes 1310752 | tf_op jit(solution)/shard_map/ppermute | solution.py:477
  69.4 1.7 %add_remote.4.total = bf16[512,2560]{1,0:T(8,128)(2,1)} custom-call(bf16[512,2560]{1,0:T(8,128)(2,1)S(1)} %project.1.refs_0_.terms, bf16[512,640]{1,0:T(8,128)(2,1)S(1)} %gate.1.rest_0_.refs_1_.mine, bf16[512,640]{1,0:T(8,128)(2,1)S(1)} %collective-permute-done.10.refs_2_.other, ...), custom_call_target="tpu_custom_call", output_to_operand_aliasing={{}: (4, {})} | custom-call | flops 1024 | bytes 1024 | tf_op jit(solution)/shard_map/add_remote/pallas_call | solution.py:425
  71.1 2.3 %collective-permute-done.11.weight = bf16[1280,512]{1,0:T(8,128)(2,1)S(1)} collective-permute-done((bf16[1280,512]{1,0:T(8,128)(2,1)S(1)}, bf16[1280,512]{1,0:T(8,128)(2,1)S(1)}, u32[]{:S(2)}, u32[]{:S(2)}) %collective-permute-start.11) | collective-permute-done | bytes 1310752 | tf_op jit(solution)/shard_map/ppermute | solution.py:479
  73.3 1.7 %add_remote.5.total = bf16[512,2560]{1,0:T(8,128)(2,1)} custom-call(bf16[512,2560]{1,0:T(8,128)(2,1)S(1)} %project.1.refs_0_.terms, bf16[512,640]{1,0:T(8,128)(2,1)S(1)} %gate.1.rest_0_.refs_1_.mine, bf16[512,640]{1,0:T(8,128)(2,1)S(1)} %collective-permute-done.10.refs_2_.other, ...), custom_call_target="tpu_custom_call", output_to_operand_aliasing={{}: (4, {})} | custom-call | flops 1024 | bytes 1024 | tf_op jit(solution)/shard_map/add_remote/pallas_call | solution.py:425
  75.0 1.5 %collective-permute-done.9.came = bf16[512,1024]{1,0:T(8,128)(2,1)S(1)} collective-permute-done((bf16[512,1024]{1,0:T(8,128)(2,1)S(1)}, bf16[512,1024]{1,0:T(8,128)(2,1)S(1)}, u32[]{:S(2)}, u32[]{:S(2)}) %collective-permute-start.9) | collective-permute-done | bytes 1048608 | tf_op jit(solution)/shard_map/ppermute | solution.py:485
  (17 shorter events, 3.1 us)
Async XLA Ops:
  2.6 8.6 %collective-permute-start = (bf16[1152,640]{1,0:T(8,128)(2,1)S(1)}, bf16[1152,640]{1,0:T(8,128)(2,1)S(1)}, u32[]{:S(2)}, u32[]{:S(2)}) collective-permute-start(bf16[1152,640]{1,0:T(8,128)(2,1)S(1)} %get-tuple-element.18), channel_id=1, source_target_pairs={{0,1},{1,0},{2,3},{3,2},{4,5},{5,4},{6,7},{7,6},{8,9},{9,8},{10,11... | collective-permute-start | bytes 4423688 | tf_op jit(solution)/shard_map/ppermute | solution.py:464
  3.1 23.0 %collective-permute-start.1 = (bf16[256,640]{1,0:T(8,128)(2,1)S(1)}, bf16[256,640]{1,0:T(8,128)(2,1)S(1)}, u32[]{:S(2)}, u32[]{:S(2)}) collective-permute-start(bf16[256,640]{1,0:T(8,128)(2,1)S(1)} %get-tuple-element.24), channel_id=1, source_target_pairs={{0,4},{4,8},{8,12},{12,0},{1,5},{5,9},{9,13},{13,1},{2,6},{6,10},{... | collective-permute-start | bytes 983048 | tf_op jit(solution)/shard_map/ppermute | solution.py:462
  5.8 24.5 %collective-permute-start.2 = (bf16[256,640]{1,0:T(8,128)(2,1)S(1)}, bf16[256,640]{1,0:T(8,128)(2,1)S(1)}, u32[]{:S(2)}, u32[]{:S(2)}) collective-permute-start(bf16[256,640]{1,0:T(8,128)(2,1)S(1)} %get-tuple-element.25), channel_id=1, source_target_pairs={{0,8},{4,12},{8,0},{12,4},{1,9},{5,13},{9,1},{13,5},{2,10},{6,14},... | collective-permute-start | bytes 983048 | tf_op jit(solution)/shard_map/ppermute | solution.py:462
  8.4 21.9 %collective-permute-start.3 = (bf16[256,640]{1,0:T(8,128)(2,1)S(1)}, bf16[256,640]{1,0:T(8,128)(2,1)S(1)}, u32[]{:S(2)}, u32[]{:S(2)}) collective-permute-start(bf16[256,640]{1,0:T(8,128)(2,1)S(1)} %get-tuple-element.26), channel_id=1, source_target_pairs={{0,12},{4,0},{8,4},{12,8},{1,13},{5,1},{9,5},{13,9},{2,14},{6,2},{... | collective-permute-start | bytes 983048 | tf_op jit(solution)/shard_map/ppermute | solution.py:462
  9.7 31.7 %collective-permute-start.5 = (bf16[1280,512]{1,0:T(8,128)(2,1)S(1)}, bf16[1280,512]{1,0:T(8,128)(2,1)S(1)}, u32[]{:S(2)}, u32[]{:S(2)}) collective-permute-start(bf16[1280,512]{1,0:T(8,128)(2,1)S(1)} %get-tuple-element.28), channel_id=1, source_target_pairs={{0,2},{2,0},{1,3},{3,1},{4,6},{6,4},{5,7},{7,5},{8,10},{10,8},{9,1... | collective-permute-start | bytes 3932168 | tf_op jit(solution)/shard_map/ppermute | solution.py:463
  30.3 1.9 %collective-permute-start.4 = (bf16[384,640]{1,0:T(8,128)(2,1)S(1)}, bf16[384,640]{1,0:T(8,128)(2,1)S(1)}, u32[]{:S(2)}, u32[]{:S(2)}) collective-permute-start(bf16[384,640]{1,0:T(8,128)(2,1)S(1)} %pass_on.1.rest_4_), channel_id=1, source_target_pairs={{0,1},{1,0},{2,3},{3,2},{4,5},{5,4},{6,7},{7,6},{8,9},{9,8},{10,11... | collective-permute-start | bytes 1474568 | tf_op jit(solution)/shard_map/ppermute | solution.py:469
  33.7 13.0 %collective-permute-start.8 = (bf16[512,640]{1,0:T(8,128)(2,1)S(1)}, bf16[512,640]{1,0:T(8,128)(2,1)S(1)}, u32[]{:S(2)}, u32[]{:S(2)}) collective-permute-start(bf16[512,640]{1,0:T(8,128)(2,1)S(1)} %far_last.1.after.mine), channel_id=1, source_target_pairs={{0,1},{1,0},{2,3},{3,2},{4,5},{5,4},{6,7},{7,6},{8,9},{9,8},{10,11... | collective-permute-start | bytes 1966088 | tf_op jit(solution)/shard_map/ppermute | solution.py:476
  33.9 21.6 %collective-permute-start.7 = (bf16[512,640]{1,0:T(8,128)(2,1)S(1)}, bf16[512,640]{1,0:T(8,128)(2,1)S(1)}, u32[]{:S(2)}, u32[]{:S(2)}) collective-permute-start(bf16[512,640]{1,0:T(8,128)(2,1)S(1)} %far_last.1.after.mine), channel_id=1, source_target_pairs={{0,2},{2,0},{1,3},{3,1},{4,6},{6,4},{5,7},{7,5},{8,10},{10,8},{9,1... | collective-permute-start | bytes 1966088 | tf_op jit(solution)/shard_map/ppermute | solution.py:475
  41.4 28.0 %collective-permute-start.12 = (bf16[1280,512]{1,0:T(8,128)(2,1)S(1)}, bf16[1280,512]{1,0:T(8,128)(2,1)S(1)}, u32[]{:S(2)}, u32[]{:S(2)}) collective-permute-start(bf16[1280,512]{1,0:T(8,128)(2,1)S(1)} %collective-permute-done.5.array.refs_3_), channel_id=1, source_target_pairs={{0,16},{16,0},{1,17},{17,1},{2,18},{18,2},{3,19},{19,3},{4,20},{20... | collective-permute-start | bytes 3932168 | tf_op jit(solution)/shard_map/ppermute | solution.py:477
  43.0 30.3 %collective-permute-start.11 = (bf16[1280,512]{1,0:T(8,128)(2,1)S(1)}, bf16[1280,512]{1,0:T(8,128)(2,1)S(1)}, u32[]{:S(2)}, u32[]{:S(2)}) collective-permute-start(bf16[1280,512]{1,0:T(8,128)(2,1)S(1)} %copied.1.rest_8_), channel_id=1, source_target_pairs={{0,4},{4,0},{8,12},{12,8},{1,5},{5,1},{9,13},{13,9},{2,6},{6,2},{1... | collective-permute-start | bytes 3932168 | tf_op jit(solution)/shard_map/ppermute | solution.py:479
  48.2 28.3 %collective-permute-start.9 = (bf16[512,1024]{1,0:T(8,128)(2,1)S(1)}, bf16[512,1024]{1,0:T(8,128)(2,1)S(1)}, u32[]{:S(2)}, u32[]{:S(2)}) collective-permute-start(bf16[512,1024]{1,0:T(8,128)(2,1)S(1)} %project_unshared.1.refs_1_), channel_id=1, source_target_pairs={{0,2},{2,0},{1,3},{3,1},{4,6},{6,4},{5,7},{7,5},{8,10},{10,8},{9,1... | collective-permute-start | bytes 3145736 | tf_op jit(solution)/shard_map/ppermute | solution.py:485
  48.8 6.6 %collective-permute-start.6 = (bf16[512,640]{1,0:T(8,128)(2,1)S(1)}, bf16[512,640]{1,0:T(8,128)(2,1)S(1)}, u32[]{:S(2)}, u32[]{:S(2)}) collective-permute-start(bf16[512,640]{1,0:T(8,128)(2,1)S(1)} %near.1.rest_0_.mine), channel_id=1, source_target_pairs={{0,1},{1,0},{2,3},{3,2},{4,5},{5,4},{6,7},{7,6},{8,9},{9,8},{10,11... | collective-permute-start | bytes 1966088 | tf_op jit(solution)/shard_map/ppermute | solution.py:482
  55.5 4.4 %collective-permute-start.10 = (bf16[512,640]{1,0:T(8,128)(2,1)S(1)}, bf16[512,640]{1,0:T(8,128)(2,1)S(1)}, u32[]{:S(2)}, u32[]{:S(2)}) collective-permute-start(bf16[512,640]{1,0:T(8,128)(2,1)S(1)} %gate.1.rest_0_.refs_1_.mine), channel_id=1, source_target_pairs={{0,1},{1,0},{2,3},{3,2},{4,5},{5,4},{6,7},{7,6},{8,9},{9,8},{10,11... | collective-permute-start | bytes 1966088 | tf_op jit(solution)/shard_map/ppermute | solution.py:487
